TPU v7x, 32 devices: a whole 2x2x4 slice. The times are simulated.
32 devices in a mesh: gx: 4 (over y, x), gy: 4 (over z), gz: 2 (over core).
Axes of the slice: x: 2, y: 2, z: 4, core: 2. Of those that a mesh axis runs over, the one named last changes fastest.
Arguments:
- nodal_field: float32 [128, 512, 512], P('gx', 'gy', 'gz'), may hold values from -6 to 6
- spacing_x: float32 [128], replicated, may hold values from 0.5 to 2
- spacing_z: float32 [512], replicated, may hold values from 0.5 to 2
- operator_x: float32 [64, 16], P('gx'), may hold values from -1.5 to 1.5
- persist_x: float32 [64], P('gx'), may hold values from 0.6 to 1
- operator_z: float32 [256, 128], P('gz'), may hold values from -0.5 to 0.5
- persist_z: float32 [256], P('gz'), may hold values from 0.6 to 1
- receivers: int32 [16384, 1], P(('gx', 'gy', 'gz')), may hold values from 0 to 7; in each aligned block of 512 rows (0 to 511, 512 to 1023, ...) at most 128 rows name the same one
Outputs:
- detail_x: float32 [64, 512, 512], P('gx', 'gy', 'gz')
- detail_z: float32 [64, 512, 256], P('gx', 'gy', 'gz')
- received: float32 [32, 8, 128, 2, 4, 128], P(('gx', 'gy', 'gz'))
Inputs may be any that keep to these rules, and one draw needn't show every extreme that they name: `receivers`: each row names the receiving device of one kept block among the 8 devices with the same gx index, in (gy, gz) row-major order; of the 512 blocks of one device at most 128 name the same receiver, and that bound is reached.
All inputs are finite; a program needn't handle non-finite values.
Results may differ from a plain program's by a relative error of at most 0.00008.
Values sent between devices are 32-bit elements; how exact they have to be, the bound alone decides.
A program may use at most 64 MiB of HBM per device.

v0:
```python
import functools

import jax
import jax.numpy as jnp
from jax import lax
from jax.experimental import pallas as pl
from jax.experimental.pallas import tpu as pltpu
from jax.sharding import PartitionSpec as P

LINES = 4
MESH = pl.DeviceIdType.MESH
HIGHEST = lax.Precision.HIGHEST
LIMIT = 56 * 1024 * 1024


def neighbours(spacing):
    count = spacing.shape[1]
    parts, rest = [], spacing
    for _ in range(3):
        part = rest.astype(jnp.bfloat16).astype(jnp.float32)
        parts.append(part)
        rest = rest - part
    kind = lax.broadcasted_iota(jnp.int32, (16, count), 0)
    stacked = jnp.zeros((16, count), jnp.float32)
    for k, part in enumerate(parts):
        stacked = jnp.where(kind == k, part, stacked)
    row = lax.broadcasted_iota(jnp.int32, (count, 128), 0)
    twice = 2 * lax.broadcasted_iota(jnp.int32, (count, 128), 1)
    chosen = [
        jnp.dot(
            stacked.astype(jnp.bfloat16),
            jnp.where(row == twice + shift, 1.0, 0.0).astype(jnp.bfloat16),
            preferred_element_type=jnp.float32,
        )
        for shift in (0, 1, -2, -1)
    ]
    return [jnp.sum(one, axis=0, keepdims=True) for one in chosen]


def coefficients(even, odd, even_before, odd_before):
    def parts(even, odd):
        total = even + odd
        total = jnp.where(total > 0, total, 1.0)
        return odd / total, even / total

    return (
        parts(even, odd) + (0.5 * even, 0.5 * odd_before) + parts(even_before, odd_before)
    )


def prepare_kernel(
    spacing_x, spacing_z, factor, gain, targets, scalars, coefz, placed, header, *, group,
    capacity, listed,
):
    half = factor.shape[0]
    scalars[...] = jnp.zeros_like(scalars)
    for k, row in enumerate(coefficients(*neighbours(spacing_x[...]))):
        scalars[k : k + 1, :] = row
    scalars[8 : 8 + half, 0:half] = factor[...]
    scalars[8 + half : 9 + half, 0:half] = gain[...]

    me = lax.axis_index("gz")
    width = coefz.shape[1]
    start = pl.multiple_of(me * (2 * width), 2 * width)
    here = neighbours(spacing_z[:, pl.ds(start, 2 * width)])
    earlier = pl.multiple_of(jnp.maximum(start - width, 0), width)
    previous = spacing_z[:, pl.ds(earlier, width)]
    lane = lax.broadcasted_iota(jnp.int32, (1, width), 1)
    inside = jnp.where(me > 0, 1.0, 0.0)
    first = lane == 0
    even_before = jnp.where(first, inside * previous[:, width - 2 : width - 1], here[2])
    odd_before = jnp.where(first, inside * previous[:, width - 1 : width], here[3])
    coefz[...] = jnp.zeros_like(coefz)
    for k, row in enumerate(coefficients(here[0], here[1], even_before, odd_before)):
        coefz[k : k + 1, :] = row

    blocks = targets.shape[1]
    member = lax.broadcasted_iota(jnp.int32, (group, blocks), 0)
    named = jnp.where(member == targets[...], 1.0, 0.0)
    before = lax.broadcasted_iota(jnp.int32, (blocks, blocks), 0)
    after = lax.broadcasted_iota(jnp.int32, (blocks, blocks), 1)
    counted = jnp.dot(
        named.astype(jnp.bfloat16),
        jnp.where(before < after, 1.0, 0.0).astype(jnp.bfloat16),
        preferred_element_type=jnp.float32,
    )
    slot = jnp.sum(named * counted, axis=0, keepdims=True).astype(jnp.int32)
    place = targets[...] * capacity + slot
    header[...] = jnp.zeros_like(header)
    if listed:
        direct = capacity // 2
        there = 1 - lax.axis_index("gy") // 2
        tally = jnp.sum(named, axis=1, keepdims=True)
        kind = lax.broadcasted_iota(jnp.int32, (group, 1), 0)
        more = jnp.where(kind // 4 == there, jnp.maximum(tally - direct, 0.0), 0.0)
        ahead = jnp.sum(jnp.where(member < targets[...], more, 0.0), axis=0, keepdims=True)
        listing = group * capacity + 1 - direct + ahead.astype(jnp.int32) + slot
        place = jnp.where((targets[...] // 4 == there) & (slot >= direct), listing, place)
        side = lax.broadcasted_iota(jnp.int32, (group, 128), 0)
        across = lax.broadcasted_iota(jnp.int32, (group, 128), 1)
        header[0:1, :] = jnp.sum(jnp.where(side == across, more, 0.0), axis=0, keepdims=True)
        scalars[9 + half : 10 + half, :] = jnp.sum(more, axis=0, keepdims=True) + jnp.zeros(
            (1, 128), jnp.float32
        )
    placed[...] = place


class Table:
    def __init__(self, scalars):
        self.scalars = scalars

    def __getitem__(self, place):
        return self.scalars[8 + place[0], place[1]]


def exchange_first(
    count, over, scalars, hbm_nodes, out, most, nodes, left, right, send, tails, needs, wants,
    send_sem, recv_sem, need_send, need_recv, want_send, want_recv, load_sem,
):
    me, row = lax.axis_index("gx"), lax.axis_index("gy")
    load = pltpu.make_async_copy(hbm_nodes, nodes, load_sem)
    load.start()
    half = nodes.shape[0] // 2
    lines = nodes.shape[1]
    barrier = pltpu.get_barrier_semaphore()
    for d in range(1, count):
        pl.semaphore_signal(
            barrier, inc=1, device_id={"gx": lax.rem(me + d, count)}, device_id_type=MESH
        )
    for d in range(1, over):
        pl.semaphore_signal(
            barrier, inc=1, device_id={"gy": lax.rem(row + d, over)}, device_id_type=MESH
        )

    def coef(kind, k):
        return scalars[kind, me * half + k]

    factor = Table(scalars)
    gain_last = scalars[8 + half, half - 1]
    needs[0] = jnp.full(needs.shape[1:], scalars[9 + half, 0], jnp.float32)
    load.wait()

    last = half - 1
    send[1, pl.ds(0, lines), :] = nodes[2 * last + 1] - coef(0, last) * nodes[2 * last]
    pl.semaphore_wait(barrier, count + over - 2)

    to_right = pltpu.make_async_remote_copy(
        src_ref=send.at[1, pl.ds(0, lines)], dst_ref=left, send_sem=send_sem.at[0], recv_sem=recv_sem.at[0],
        device_id={"gx": lax.rem(me + 1, count)}, device_id_type=MESH,
    )
    to_left = pltpu.make_async_remote_copy(
        src_ref=nodes.at[0], dst_ref=right, send_sem=send_sem.at[1], recv_sem=recv_sem.at[1],
        device_id={"gx": lax.rem(me + count - 1, count)}, device_id_type=MESH,
    )

    @pl.when(me < count - 1)
    def _():
        to_right.start()

    @pl.when(me > 0)
    def _():
        to_left.start()

    small = []
    for d in range(1, count):
        small.append(
            pltpu.make_async_remote_copy(
                src_ref=needs.at[0], dst_ref=needs.at[d],
                send_sem=need_send.at[d], recv_sem=need_recv.at[d],
                device_id={"gx": lax.rem(me + d, count)}, device_id_type=MESH,
            )
        )
        small[-1].start()

    weights = []
    for k in range(half):
        weight = factor[last, k] * coef(2, k)
        if k < last:
            weight = weight + factor[last, k + 1] * coef(3, k + 1)
        weights.append(weight)
    edge = factor[last, 0] * coef(3, 0)

    def chunk(i, carry):
        rows = pl.ds(pl.multiple_of(i * 8, 8), 8)
        even = nodes[0, rows, :]
        value = (-edge * coef(5, 0)) * even
        for k in range(half):
            detail = nodes[2 * k + 1, rows, :] - coef(0, k) * even
            if k < last:
                even = nodes[2 * k + 2, rows, :]
                detail = detail - coef(1, k) * even
            value = value + weights[k] * detail
        send[0, rows, :] = value
        return carry

    lax.fori_loop(0, lines // 8, chunk, 0)
    for one in small:
        one.wait_recv()
    wants[0] = jnp.max(needs[...], axis=0)
    for d in range(1, over):
        small.append(
            pltpu.make_async_remote_copy(
                src_ref=wants.at[0], dst_ref=wants.at[d],
                send_sem=want_send.at[d], recv_sem=want_recv.at[d],
                device_id={"gy": lax.rem(row + d, over)}, device_id_type=MESH,
            )
        )
        small[-1].start()

    @pl.when(me == 0)
    def _():
        left[...] = jnp.zeros_like(left)

    @pl.when(me == count - 1)
    def _():
        right[...] = jnp.zeros_like(right)

    @pl.when(me > 0)
    def _():
        to_right.wait_recv()

    @pl.when(me < count - 1)
    def _():
        to_left.wait_recv()

    end = -(factor[last, last] * coef(2, last)) * coef(1, last)
    own = send.at[0]
    own[pl.ds(0, lines), :] = own[pl.ds(0, lines), :] + edge * left[...] + end * right[...]
    own[pl.ds(lines, 8), :] = jnp.full((8, own.shape[1]), gain_last, jnp.float32)

    copies = []
    for d in range(1, count):
        copies.append(
            pltpu.make_async_remote_copy(
                src_ref=tails.at[0], dst_ref=tails.at[d],
                send_sem=send_sem.at[1 + d], recv_sem=recv_sem.at[1 + d],
                device_id={"gx": lax.rem(me + d, count)}, device_id_type=MESH,
            )
        )
    tails[0] = own[...]
    for d in range(1, count):

        @pl.when(me + d < count)
        def _(d=d):
            copies[d - 1].start()

    out[0] = left[...]
    out[1] = right[...]
    out[2] = jnp.zeros_like(left)
    for d in range(count - 1, 0, -1):

        @pl.when(me >= d)
        def _(d=d):
            copies[d - 1].wait_recv()
            out[2] = (
                tails[d, pl.ds(0, lines), :]
                + jnp.max(tails[d, pl.ds(lines, 8), :], axis=0, keepdims=True) * out[2]
            )

    for one in small[count - 1 :]:
        one.wait_recv()
    most[...] = jnp.max(wants[...], axis=0)
    for one in small:
        one.wait_send()

    @pl.when(me < count - 1)
    def _():
        to_right.wait_send()

    @pl.when(me > 0)
    def _():
        to_left.wait_send()

    for d in range(1, count):

        @pl.when(me + d < count)
        def _(d=d):
            copies[d - 1].wait_send()


def loads(coefz):
    width = coefz.shape[1]
    row = lax.broadcasted_iota(jnp.int32, (2 * width, width), 0)
    twice = 2 * lax.broadcasted_iota(jnp.int32, (2 * width, width), 1)
    a, b, half_even, half_odd, a_before, b_before = [coefz[k : k + 1, :] for k in range(6)]
    zero = jnp.zeros((2 * width, width), jnp.float32)
    detail = jnp.where(row == twice, -a, zero)
    detail = jnp.where(row == twice + 1, 1.0, detail)
    detail = jnp.where(row == twice + 2, -b, detail)
    earlier = jnp.where(row == twice - 2, -a_before, zero)
    earlier = jnp.where(row == twice - 1, 1.0, earlier)
    earlier = jnp.where(row == twice, -b_before, earlier)
    return detail, half_even * detail + half_odd * earlier, row == twice


def first_kernel(
    nodes, planes, most, scalars, coefz, factor_z, gain_z, detail, coarse, payload, weights,
    *, count,
):
    me = lax.axis_index("gx")
    half = detail.shape[0]
    factor = Table(scalars)

    def coef(row, k):
        return scalars[row, me * half + k]

    width = factor_z.shape[0]

    @pl.when(pl.program_id(0) == 0)
    def _():
        load = loads(coefz)[1]
        tail = lax.dot_general(
            factor_z[pl.ds(width - 8, 8), :], load, (((1,), (1,)), ((), ())), precision=HIGHEST
        )
        lane = lax.broadcasted_iota(jnp.int32, (1, 2 * width), 1)
        a_last = coefz[0:1, width - 1 : width]
        weights[...] = jnp.zeros_like(weights)
        weights[0:1, :] = jnp.where(lane == 0, 1.0, 0.0)
        weights[1:2, :] = jnp.where(
            lane == 2 * width - 2, -a_last, jnp.where(lane == 2 * width - 1, 1.0, 0.0)
        )
        weights[2:3, :] = tail[7:8, :]

    for i in range(nodes.shape[1] // 8):
        rows = pl.ds(i * 8, 8)
        even = [nodes[2 * k, rows, :] for k in range(half)]
        before = planes[0, rows, :] - coef(5, 0) * even[0]
        load = []
        for k in range(half):
            after = even[k + 1] if k + 1 < half else planes[1, rows, :]
            value = nodes[2 * k + 1, rows, :] - coef(0, k) * even[k] - coef(1, k) * after
            detail[k, rows, :] = value
            load.append(coef(2, k) * value + coef(3, k) * before)
            before = value
        for k in range(half):
            value = nodes[2 * k, rows, :] + scalars[8 + half, k] * planes[2, rows, :]
            for j in range(half):
                value = value + factor[k, j] * load[j]
            coarse[k, rows, :] = value

    lines = coarse[...].reshape(half * coarse.shape[1], coarse.shape[2])
    sent = lax.dot_general(
        weights[...], lines, (((1,), (1,)), ((), ())), precision=HIGHEST
    )
    kind = lax.broadcasted_iota(jnp.int32, sent.shape, 0)
    end_gain = gain_z[0:1, width - 1 : width]
    end_first = factor_z[width - 1 : width, 0:1] * coefz[3:4, 0:1]
    end_last = -(
        factor_z[width - 1 : width, width - 1 : width]
        * coefz[2:3, width - 1 : width]
        * coefz[1:2, width - 1 : width]
    )
    sent = jnp.where(kind == 3, end_gain, sent)
    sent = jnp.where(kind == 4, end_first, sent)
    sent = jnp.where(kind == 5, end_last, sent)
    sent = jnp.where(kind == 6, most[0:1, 0:1], sent)
    payload[0] = sent


def third_kernel(
    placed, coarse, gathered, coefz, factor_z, gain_z, header, detail, outgoing, level, matrix,
    update, tiles, *, count, chunks, levels, head,
):
    me = lax.axis_index("gz")
    step = pl.program_id(0)
    width = factor_z.shape[0]

    @pl.when(step == 0)
    def _():
        outgoing[...] = jnp.zeros_like(outgoing)
        outgoing[head] = header[...]
        need = jnp.max(gathered[:, 0, 6:7, :])
        level[0] = sum((need > sent).astype(jnp.int32) for sent in levels)
        detail_of, load_of, is_even = loads(coefz)
        solved = lax.dot_general(
            load_of, factor_z[...], (((1,), (1,)), ((), ())), precision=HIGHEST
        )
        matrix[:, 0:width] = jnp.where(is_even, 1.0, 0.0) + solved
        matrix[:, width:] = detail_of
        turned = factor_z[...].T
        b_last = coefz[1:2, width - 1 : width]
        lane = lax.broadcasted_iota(jnp.int32, (1, width), 1)
        update[...] = jnp.zeros_like(update)
        update[0:1, 0:width] = -turned[width - 1 : width, :] * (
            coefz[2:3, width - 1 : width] * b_last
        )
        update[0:1, width:] = jnp.where(lane == width - 1, -b_last, 0.0)
        update[1:2, 0:width] = turned[0:1, :] * coefz[3:4, 0:1]
        update[2:3, 0:width] = gain_z[...]

    def heard(p, row):
        return gathered[p, 0, row : row + 1, :]

    empty = jnp.zeros_like(heard(0, 0))
    right, left, carry = empty, empty, empty
    for p in range(count):
        right = jnp.where(me + 1 == p, heard(p, 0), right)
        left = jnp.where(me - 1 == p, heard(p, 1), left)
        if p < count - 1:
            tail = heard(p, 2) + heard(p, 5) * heard(p + 1, 0) + heard(p, 3) * carry
            if p > 0:
                tail = tail + heard(p, 4) * heard(p - 1, 1)
            carry = jnp.where(p < me, tail, carry)
    kind = lax.broadcasted_iota(jnp.int32, (8, empty.shape[1]), 0)
    edges = jnp.where(kind == 0, right, jnp.where(kind == 1, left, jnp.where(kind == 2, carry, 0.0)))

    rows = coarse.shape[0] * coarse.shape[1]
    lines = coarse[...].reshape(rows, coarse.shape[2])
    result = jnp.dot(lines, matrix[...], precision=HIGHEST) + lax.dot_general(
        edges, update[...], (((0,), (0,)), ((), ())), precision=HIGHEST
    )
    upper = result[:, :width].reshape(rows // 8, 8, width)
    lower = result[:, width:].reshape(rows // 8, 8, width)
    detail[...] = result[:, width:].reshape(detail.shape)
    top = lax.broadcasted_iota(jnp.int32, upper.shape, 1) < LINES
    tiles[0] = jnp.where(top, upper, pltpu.roll(lower, LINES, 1))
    tiles[1] = jnp.where(top, pltpu.roll(upper, LINES, 1), lower)
    eights = coarse.shape[1] // 8

    def scatter(x, carry):
        for j in range(eights):
            for half in range(2):
                block = x * (2 * eights * chunks) + step * (2 * eights) + 2 * j + half
                outgoing[placed[0, block]] = tiles[half, x * eights + j]
        return carry

    lax.fori_loop(0, coarse.shape[0], scatter, 0)


def deliver_kernel(n_gy, n_gz, outgoing, received, send_sem, recv_sem, own_sem):
    gy, gz = lax.axis_index("gy"), lax.axis_index("gz")
    me = gy * n_gz + gz
    shifts = [
        (dy, dz) for dy in range(n_gy) for dz in range(n_gz) if dy + dz > 0
    ]
    shifts.sort(key=lambda shift: -min(shift[0], n_gy - shift[0]))
    barrier = pltpu.get_barrier_semaphore()
    targets = []
    for dy, dz in shifts:
        there = (lax.rem(gy + dy, n_gy), lax.rem(gz + dz, n_gz))
        targets.append(there)
        pl.semaphore_signal(
            barrier, inc=1, device_id={"gy": there[0], "gz": there[1]}, device_id_type=MESH
        )
    own = pltpu.make_async_copy(outgoing.at[me], received.at[me], own_sem)
    own.start()
    pl.semaphore_wait(barrier, len(shifts))
    copies = []
    for k, there in enumerate(targets):
        copy = pltpu.make_async_remote_copy(
            src_ref=outgoing.at[there[0] * n_gz + there[1]],
            dst_ref=received.at[me],
            send_sem=send_sem.at[k],
            recv_sem=recv_sem.at[k],
            device_id={"gy": there[0], "gz": there[1]},
            device_id_type=MESH,
        )
        copy.start()
        copies.append(copy)
    own.wait()
    for copy in copies:
        copy.wait()


def spread_kernel(sent, outgoing, received, lists, send_sem, recv_sem, own_sem):
    gy, gz = lax.axis_index("gy"), lax.axis_index("gz")
    half, place = gy // 2, lax.rem(gy, 2)
    me = gy * 2 + gz
    capacity = received.shape[1]

    def at(step):
        h, y, z = step
        there_half = 1 - half if h else half
        there_place = 1 - place if y else place
        return there_half * 2 + there_place, 1 - gz if z else gz

    steps = [(h, y, z) for h in (0, 1) for y in (0, 1) for z in (0, 1) if h + y + z]
    barrier = pltpu.get_barrier_semaphore()
    for step in steps:
        there = at(step)
        pl.semaphore_signal(
            barrier, inc=1, device_id={"gy": there[0], "gz": there[1]}, device_id_type=MESH
        )
    own = pltpu.make_async_copy(
        outgoing.at[pl.ds(me * capacity, capacity)], received.at[me], own_sem
    )
    own.start()
    pl.semaphore_wait(barrier, len(steps))

    def copy(k, step, source, target):
        there = at(step)
        return pltpu.make_async_remote_copy(
            src_ref=source, dst_ref=target, send_sem=send_sem.at[k], recv_sem=recv_sem.at[k],
            device_id={"gy": there[0], "gz": there[1]}, device_id_type=MESH,
        )

    def direct(step):
        there = at(step)
        count = capacity // 2 if step[0] else capacity
        return copy(
            steps.index(step), step,
            outgoing.at[pl.ds((there[0] * 2 + there[1]) * capacity, count)],
            received.at[me, pl.ds(0, count)],
        )

    mine, beside = place * 2 + gz, (1 - place) * 2 + gz
    rows = pl.ds(0, 1 + sent)
    tail = pl.ds(received.shape[0] * capacity, 1 + sent)
    across = copy(7, (1, 0, 0), outgoing.at[tail], lists.at[mine, rows])
    along = copy(8, (0, 1, 0), lists.at[mine, rows], lists.at[mine, rows])
    to_core = copy(9, (0, 0, 1), lists.at[mine, rows], lists.at[mine, rows])
    to_core_too = copy(10, (0, 0, 1), lists.at[beside, rows], lists.at[beside, rows])
    early = [direct((0, 1, 0)), direct((0, 0, 1))]
    late = [direct(step) for step in ((1, 0, 0), (1, 0, 1), (1, 1, 0), (1, 1, 1), (0, 1, 1))]
    across.start()
    for one in early:
        one.start()
    across.wait_recv()
    along.start()
    to_core.start()
    for one in late:
        one.start()
    along.wait_recv()
    to_core_too.start()
    own.wait()
    across.wait_send()
    along.wait_send()
    for one in early + late + [to_core, to_core_too]:
        one.wait()


def gather_kernel(sent, base, hbm_lists, received, lists, tiles, sems):
    direct = tiles.shape[1] // 2
    half = lax.axis_index("gy") // 2
    me = lax.axis_index("gy") * 2 + lax.axis_index("gz")
    rows = pl.ds(0, 1 + sent)
    near = [half * 4 + k for k in range(4)]
    far = [(1 - half) * 4 + k for k in range(4)]
    low = pl.ds(0, direct)
    whole = [
        pltpu.make_async_copy(base.at[near[k]], tiles.at[k], sems.at[0, k]) for k in range(4)
    ]
    listed = [
        pltpu.make_async_copy(hbm_lists.at[k, rows], lists.at[k, rows], sems.at[1, k])
        for k in range(4)
    ]
    part = [
        pltpu.make_async_copy(base.at[far[k], low], tiles.at[4 + k, low], sems.at[2, k])
        for k in range(4)
    ]
    stores = [
        pltpu.make_async_copy(tiles.at[k], received.at[(near + far)[k]], sems.at[3 + k // 4, k % 4])
        for k in range(8)
    ]
    for one in whole + listed + part:
        one.start()
    for k in range(4):
        whole[k].wait()
        stores[k].start()
    for k in range(4):
        listed[k].wait()
        part[k].wait()
        header = lists[k, 0, 0:1, :]
        lane = lax.broadcasted_iota(jnp.int32, header.shape, 1)
        start = jnp.sum(jnp.where((lane >= half * 4) & (lane < me), header, 0.0))
        count = jnp.sum(jnp.where(lane == me, header, 0.0)).astype(jnp.int32)
        later = lists[k, pl.ds(1 + start.astype(jnp.int32), direct)]
        slot = lax.broadcasted_iota(jnp.int32, later.shape, 0)
        tiles[4 + k, pl.ds(direct, direct)] = jnp.where(slot < count, later, 0.0)
        stores[4 + k].start()
    for one in stores:
        one.wait()


def spread(outgoing, group, room, levels, level):
    capacity = (outgoing.shape[0] - room - 1) // group
    tile = outgoing.shape[1:]
    def branch(number, sent):
        def run(outgoing):
            base, lists = pl.pallas_call(
                functools.partial(spread_kernel, sent),
                out_shape=[
                    jax.ShapeDtypeStruct((group, capacity) + tile, jnp.float32),
                    jax.ShapeDtypeStruct((group // 2, room + 1) + tile, jnp.float32),
                ],
                in_specs=[pl.BlockSpec(memory_space=pl.ANY)],
                out_specs=[pl.BlockSpec(memory_space=pl.ANY)] * 2,
                scratch_shapes=[
                    pltpu.SemaphoreType.DMA((11,)),
                    pltpu.SemaphoreType.DMA((11,)),
                    pltpu.SemaphoreType.DMA,
                ],
                compiler_params=pltpu.CompilerParams(
                    collective_id=2 + number, has_side_effects=True
                ),
                name="spread",
            )(outgoing)
            return pl.pallas_call(
                functools.partial(gather_kernel, sent),
                in_specs=[pl.BlockSpec(memory_space=pl.ANY)] * 2,
                out_specs=pl.BlockSpec(memory_space=pltpu.HBM),
                scratch_shapes=[
                    pltpu.VMEM((group // 2, room + 1) + tile, jnp.float32),
                    pltpu.VMEM((group, capacity) + tile, jnp.float32),
                    pltpu.SemaphoreType.DMA((5, group // 2)),
                ],
                out_shape=jax.ShapeDtypeStruct(base.shape, jnp.float32),
                compiler_params=pltpu.CompilerParams(vmem_limit_bytes=LIMIT),
                name="gather",
            )(base, lists)

        return run

    branches = [branch(k, sent) for k, sent in enumerate(levels + (room,))]
    return lax.switch(level, branches, outgoing)


def local(sizes, nodes, spacing_x, spacing_z, factor_x, gain_x, factor_z, gain_z, receivers):
    n_gx, n_gy, n_gz = sizes
    length, lines, depth = nodes.shape
    half, width = length // 2, depth // 2
    group = n_gy * n_gz
    blocks = half * lines // LINES
    capacity = max(2, blocks // group * 2)
    listed = n_gy == 4 and n_gz == 2
    direct = capacity // 2
    room = group // 2 * (capacity - direct) if listed else 0
    levels = tuple(room * k // 32 for k in (12, 16, 19))
    scalars, coefz, placed, header = pl.pallas_call(
        functools.partial(prepare_kernel, group=group, capacity=capacity, listed=listed),
        out_shape=[
            jax.ShapeDtypeStruct((32, 128), jnp.float32),
            jax.ShapeDtypeStruct((8, width), jnp.float32),
            jax.ShapeDtypeStruct((1, blocks), jnp.int32),
            jax.ShapeDtypeStruct((2 * LINES, 128), jnp.float32),
        ],
        compiler_params=pltpu.CompilerParams(vmem_limit_bytes=LIMIT),
        name="prepare",
    )(
        spacing_x.reshape(1, -1), spacing_z.reshape(1, -1), factor_x, gain_x.reshape(1, -1),
        receivers.reshape(1, -1),
    )
    gain_row = gain_z.reshape(1, width)
    vmem = pl.BlockSpec(memory_space=pltpu.VMEM)
    smem = pl.BlockSpec(memory_space=pltpu.SMEM)
    hbm = pl.BlockSpec(memory_space=pl.ANY)

    planes, most = pl.pallas_call(
        functools.partial(exchange_first, n_gx, n_gy),
        out_shape=[
            jax.ShapeDtypeStruct((3, lines, depth), jnp.float32),
            jax.ShapeDtypeStruct((8, 128), jnp.float32),
        ],
        in_specs=[smem, hbm],
        out_specs=[vmem, vmem],
        scratch_shapes=[
            pltpu.VMEM((length, lines, depth), jnp.float32),
            pltpu.VMEM((lines, depth), jnp.float32),
            pltpu.VMEM((lines, depth), jnp.float32),
            pltpu.VMEM((2, lines + 8, depth), jnp.float32),
            pltpu.VMEM((n_gx, lines + 8, depth), jnp.float32),
            pltpu.VMEM((n_gx, 8, 128), jnp.float32),
            pltpu.VMEM((n_gy, 8, 128), jnp.float32),
            pltpu.SemaphoreType.DMA((n_gx + 1,)),
            pltpu.SemaphoreType.DMA((n_gx + 1,)),
            pltpu.SemaphoreType.DMA((n_gx,)),
            pltpu.SemaphoreType.DMA((n_gx,)),
            pltpu.SemaphoreType.DMA((n_gy,)),
            pltpu.SemaphoreType.DMA((n_gy,)),
            pltpu.SemaphoreType.DMA,
        ],
        compiler_params=pltpu.CompilerParams(
            collective_id=0, has_side_effects=True, vmem_limit_bytes=LIMIT
        ),
        name="exchange_first",
    )(scalars, nodes)

    chunks = 4
    rows = lines // chunks
    params = pltpu.CompilerParams(
        dimension_semantics=("arbitrary",), vmem_limit_bytes=LIMIT
    )
    detail_x, coarse_x, payload = pl.pallas_call(
        functools.partial(first_kernel, count=n_gx),
        grid=(chunks,),
        in_specs=[
            pl.BlockSpec((length, rows, depth), lambda i: (0, i, 0)),
            pl.BlockSpec((3, rows, depth), lambda i: (0, i, 0)),
            pl.BlockSpec((8, 128), lambda i: (0, 0)),
            smem,
            pl.BlockSpec((8, width), lambda i: (0, 0)),
            pl.BlockSpec((width, width), lambda i: (0, 0)),
            pl.BlockSpec((1, width), lambda i: (0, 0)),
        ],
        out_specs=[
            pl.BlockSpec((half, rows, depth), lambda i: (0, i, 0)),
            pl.BlockSpec((half, rows, depth), lambda i: (0, i, 0)),
            pl.BlockSpec((1, 8, half * rows), lambda i: (i, 0, 0)),
        ],
        out_shape=[
            jax.ShapeDtypeStruct((half, lines, depth), jnp.float32),
            jax.ShapeDtypeStruct((half, lines, depth), jnp.float32),
            jax.ShapeDtypeStruct((chunks, 8, half * rows), jnp.float32),
        ],
        scratch_shapes=[pltpu.VMEM((8, depth), jnp.float32)],
        compiler_params=params,
        name="pass_first",
    )(nodes, planes, most, scalars, coefz, factor_z, gain_row)

    gathered = lax.all_gather(payload, "gz")

    held = group * capacity + (room + 1 if listed else 1)
    detail_z, outgoing, level = pl.pallas_call(
        functools.partial(
            third_kernel, count=n_gz, chunks=chunks, levels=levels, head=group * capacity
        ),
        grid=(chunks,),
        in_specs=[
            smem,
            pl.BlockSpec((half, rows, depth), lambda i: (0, i, 0)),
            pl.BlockSpec((n_gz, 1, 8, half * rows), lambda i: (0, i, 0, 0)),
            pl.BlockSpec((8, width), lambda i: (0, 0)),
            pl.BlockSpec((width, width), lambda i: (0, 0)),
            pl.BlockSpec((1, width), lambda i: (0, 0)),
            pl.BlockSpec((2 * LINES, width), lambda i: (0, 0)),
        ],
        out_specs=[
            pl.BlockSpec((half, rows, width), lambda i: (0, i, 0)),
            pl.BlockSpec((held, 2 * LINES, width), lambda i: (0, 0, 0)),
            smem,
        ],
        out_shape=[
            jax.ShapeDtypeStruct((half, lines, width), jnp.float32),
            jax.ShapeDtypeStruct((held, 2 * LINES, width), jnp.float32),
            jax.ShapeDtypeStruct((1,), jnp.int32),
        ],
        scratch_shapes=[
            pltpu.VMEM((depth, depth), jnp.float32),
            pltpu.VMEM((8, depth), jnp.float32),
            pltpu.VMEM((2, half * rows // 8, 8, width), jnp.float32),
        ],
        compiler_params=params,
        name="pass_third",
    )(placed, coarse_x, gathered, coefz, factor_z, gain_row, header)

    if listed:
        received = spread(outgoing, group, room, levels, level[0])
    else:
        outgoing = outgoing[: group * capacity].reshape(group, capacity, 2 * LINES, width)
        received = pl.pallas_call(
            functools.partial(deliver_kernel, n_gy, n_gz),
            out_shape=jax.ShapeDtypeStruct(outgoing.shape, jnp.float32),
            in_specs=[hbm],
            out_specs=hbm,
            scratch_shapes=[
                pltpu.SemaphoreType.DMA((group - 1,)),
                pltpu.SemaphoreType.DMA((group - 1,)),
                pltpu.SemaphoreType.DMA,
            ],
            compiler_params=pltpu.CompilerParams(collective_id=1, has_side_effects=True),
            name="deliver",
        )(outgoing)
    return (
        detail_x,
        detail_z,
        received.reshape(1, group, capacity, 2, LINES, width),
    )


def solution(mesh):
    sizes = tuple(mesh.shape[axis] for axis in ("gx", "gy", "gz"))
    return jax.shard_map(
        functools.partial(local, sizes),
        mesh=mesh,
        in_specs=(
            P("gx", "gy", "gz"),
            P(),
            P(),
            P("gx", None),
            P("gx"),
            P("gz", None),
            P("gz"),
            P(("gx", "gy", "gz"), None),
        ),
        out_specs=(
            P("gx", "gy", "gz"),
            P("gx", "gy", "gz"),
            P(("gx", "gy", "gz"), None, None, None, None, None),
        ),
        check_vma=False,
    )
```

profile of v0, /device:TPU:0, one launch (start us, length us, event | category | flops | bytes accessed | tf_op | source)
XLA Modules:
  0.0 115.6 jit_solution(12905915095296439273)
XLA Ops:
  0.6 1.6 %prepare.1 = (f32[32,128]{1,0:T(8,128)}, f32[8,128]{1,0:T(8,128)}, s32[1,512]{1,0:T(1,128)}, f32[8,128]{1,0:T(8,128)}) custom-call(f32[1,128]{1,0:T(1,128)} %bitcast.20, f32[1,512]{1,0:T(1,128)} %bitcast.18, f32[16,16]{1,0:T(8,128)} %factor.1, f32[1,16]{1,0:T(1,128)} %bitcast.21, s32[1,512]{1,0:T(1,128)} %bitcast.19), custom_call_target="tpu_custom_call" | custom-call | tf_op jit(solution)/shard_map/prepare/pallas_call | solution.py:629
  2.3 20.1 %exchange_first.1 = (f32[3,128,256]{2,1,0:T(8,128)}, f32[8,128]{1,0:T(8,128)}) custom-call(f32[32,128]{1,0:T(8,128)} %get-tuple-element.33.scalars, f32[32,128,256]{2,1,0:T(8,128)} %nodes.1), custom_call_target="tpu_custom_call" | custom-call | tf_op jit(solution)/shard_map/exchange_first/pallas_call | solution.py:648
  22.4 8.9 %pass_first.1 = (f32[16,128,256]{2,1,0:T(8,128)}, f32[16,128,256]{2,1,0:T(8,128)}, f32[4,8,512]{2,1,0:T(8,128)}) custom-call(f32[32,128,256]{2,1,0:T(8,128)} %nodes.1, f32[3,128,256]{2,1,0:T(8,128)} %get-tuple-element.34.planes, f32[8,128]{1,0:T(8,128)} %get-tuple-element.35.most, f32[32,128]{1,0:T(8,128)} %get-tuple-element.33.scalars, ...), custom_call_target="tpu_custom_call" | custom-call | tf_op jit(solution)/shard_map/pass_first/pallas_call | solution.py:683
  31.3 3.3 %all-gather = f32[8,8,512]{2,1,0:T(8,128)} all-gather(f32[4,8,512]{2,1,0:T(8,128)} %get-tuple-element.40), channel_id=2, replica_groups=mesh['gx'=4,'gy'=4,'gz'=2] {'gz'}, dimensions={0}, use_global_device_ids=true | all-gather | bytes 196608 | tf_op jit(solution)/shard_map/all_gather | solution.py:710
  34.6 9.3 %pass_third.1 = (f32[16,128,128]{2,1,0:T(8,128)}, f32[1281,8,128]{2,1,0:T(8,128)}, s32[1]{0:T(128)}) custom-call(s32[1,512]{1,0:T(1,128)} %get-tuple-element.38.placed, f32[16,128,256]{2,1,0:T(8,128)} %get-tuple-element.39.coarse, f32[2,4,8,512]{3,2,1,0:T(8,128)} %bitcast.15, f32[8,128]{1,0:T(8,128)} %get-tuple-element.36.coefz, f32[128,128]{1,0:T(8,128)} %factor_z.3, ...), custom_call_target="tpu_custom_call" | custom-call | tf_op jit(solution)/shard_map/pass_third/pallas_call | solution.py:713
  44.5 71.1 %conditional.1 = (f32[1,8,128,2,4,128]{5,4,3,2,1,0:T(4,128)}) conditional(s32[]{:T(128)} %bitcast.10, f32[1281,8,128]{2,1,0:T(8,128)} %get-tuple-element.44, f32[1281,8,128]{2,1,0:T(8,128)} %get-tuple-element.44, f32[1281,8,128]{2,1,0:T(8,128)} %get-tuple-element.44, f32[1281,8,128]{2,1,0:T(8,128)} %get-tuple-element.44), branch_computations={%region_0.0_spmd, %region_1.0_spmd, %region_2.0_spmd, %region_3.0_... | conditional | bytes 8 | solution.py:615
  44.5 66.8 %spread.4 = (f32[8,128,8,128]{3,2,1,0:T(8,128)}, f32[4,257,8,128]{3,2,1,0:T(8,128)}) custom-call(f32[1281,8,128]{2,1,0:T(8,128)} %outgoing), custom_call_target="tpu_custom_call" | custom-call | tf_op jit(solution)/shard_map/cond/branch_0_fun/spread/pallas_call | solution.py:580
  111.4 4.3 %gather.4 = f32[8,128,8,128]{3,2,1,0:T(8,128)} custom-call(f32[8,128,8,128]{3,2,1,0:T(8,128)} %get-tuple-element.10.base, f32[4,257,8,128]{3,2,1,0:T(8,128)} %get-tuple-element.11.hbm_lists), custom_call_target="tpu_custom_call" | custom-call | tf_op jit(solution)/shard_map/cond/branch_0_fun/gather/pallas_call | solution.py:598
where the time goes:
time: 116 us
  Pallas kernels  111 us (96%)
  blocking collectives  3.34 us (3%)
  between operations  1.21 us (1%)
    pallas_call x1, Pallas kernels, run(): pl.pallas_call(functools.partial(spread_kernel, sent), out_shape=[jax.Sha...  66.8 us
    pallas_call x1, Pallas kernels, local(): pl.pallas_call(functools.partial(exchange_first, n_gx, n_gy), out_shape=[...  20.1 us
    pallas_call x1, Pallas kernels, local(): pl.pallas_call(functools.partial(third_kernel, count=n_gz, chunks=chunks,...  9.28 us
    pallas_call x1, Pallas kernels, local(): pl.pallas_call(functools.partial(first_kernel, count=n_gx), grid=(chunks,...  8.94 us
    pallas_call x1, Pallas kernels, run(): pl.pallas_call(functools.partial(gather_kernel, sent), in_specs=[pl.Block...  4.26 us
    all_gather x1, blocking collectives, local(): gathered = lax.all_gather(payload, 'gz')  3.34 us

commit v1 on v0

--- a/solution.py
+++ b/solution.py
@@ -118,8 +118,12 @@
     send_sem, recv_sem, need_send, need_recv, want_send, want_recv, load_sem,
 ):
     me, row = lax.axis_index("gx"), lax.axis_index("gy")
-    load = pltpu.make_async_copy(hbm_nodes, nodes, load_sem)
-    load.start()
+    ends = pl.ds(nodes.shape[0] - 2, 2)
+    body = pl.ds(0, nodes.shape[0] - 2)
+    load_ends = pltpu.make_async_copy(hbm_nodes.at[ends], nodes.at[ends], load_sem.at[0])
+    load_body = pltpu.make_async_copy(hbm_nodes.at[body], nodes.at[body], load_sem.at[1])
+    load_ends.start()
+    load_body.start()
     half = nodes.shape[0] // 2
     lines = nodes.shape[1]
     barrier = pltpu.get_barrier_semaphore()
@@ -138,7 +142,7 @@
     factor = Table(scalars)
     gain_last = scalars[8 + half, half - 1]
     needs[0] = jnp.full(needs.shape[1:], scalars[9 + half, 0], jnp.float32)
-    load.wait()
+    load_ends.wait()
 
     last = half - 1
     send[1, pl.ds(0, lines), :] = nodes[2 * last + 1] - coef(0, last) * nodes[2 * last]
@@ -149,7 +153,7 @@
         device_id={"gx": lax.rem(me + 1, count)}, device_id_type=MESH,
     )
     to_left = pltpu.make_async_remote_copy(
-        src_ref=nodes.at[0], dst_ref=right, send_sem=send_sem.at[1], recv_sem=recv_sem.at[1],
+        src_ref=hbm_nodes.at[0], dst_ref=right, send_sem=send_sem.at[1], recv_sem=recv_sem.at[1],
         device_id={"gx": lax.rem(me + count - 1, count)}, device_id_type=MESH,
     )
 
@@ -193,6 +197,7 @@
         send[0, rows, :] = value
         return carry
 
+    load_body.wait()
     lax.fori_loop(0, lines // 8, chunk, 0)
     for one in small:
         one.wait_recv()
@@ -667,7 +672,7 @@
             pltpu.SemaphoreType.DMA((n_gx,)),
             pltpu.SemaphoreType.DMA((n_gy,)),
             pltpu.SemaphoreType.DMA((n_gy,)),
-            pltpu.SemaphoreType.DMA,
+            pltpu.SemaphoreType.DMA((2,)),
         ],
         compiler_params=pltpu.CompilerParams(
             collective_id=0, has_side_effects=True, vmem_limit_bytes=LIMIT

time: 116 us -> 114 us (0.983)
  Pallas kernels: 111 us -> 109 us
    pallas_call x1, Pallas kernels: 66.8 us -> 65.2 us  [run(): pl.pallas_call(functools.partial(spread_kernel, sent), out_shape=[jax.Sha...]
where the time goes in v1:
time: 114 us
  Pallas kernels  109 us (96%)
  blocking collectives  3.34 us (3%)
  between operations  1.21 us (1%)
    pallas_call x1, Pallas kernels, run(): pl.pallas_call(functools.partial(spread_kernel, sent), out_shape=[jax.Sha...  65.2 us
    pallas_call x1, Pallas kernels, local(): pl.pallas_call(functools.partial(exchange_first, n_gx, n_gy), out_shape=[...  20.1 us
    pallas_call x1, Pallas kernels, local(): pl.pallas_call(functools.partial(third_kernel, count=n_gz, chunks=chunks,...  9.28 us
    pallas_call x1, Pallas kernels, local(): pl.pallas_call(functools.partial(first_kernel, count=n_gx), grid=(chunks,...  8.94 us
    pallas_call x1, Pallas kernels, run(): pl.pallas_call(functools.partial(gather_kernel, sent), in_specs=[pl.Block...  4.26 us
    all_gather x1, blocking collectives, local(): gathered = lax.all_gather(payload, 'gz')  3.34 us

profile of v1, /device:TPU:0, one launch (start us, length us, event | category | flops | bytes accessed | tf_op | source)
XLA Modules:
  0.0 114.0 jit_solution(4305043878060346173)
XLA Ops:
  0.6 1.6 %prepare.1 = (f32[32,128]{1,0:T(8,128)}, f32[8,128]{1,0:T(8,128)}, s32[1,512]{1,0:T(1,128)}, f32[8,128]{1,0:T(8,128)}) custom-call(f32[1,128]{1,0:T(1,128)} %bitcast.20, f32[1,512]{1,0:T(1,128)} %bitcast.18, f32[16,16]{1,0:T(8,128)} %factor.1, f32[1,16]{1,0:T(1,128)} %bitcast.21, s32[1,512]{1,0:T(1,128)} %bitcast.19), custom_call_target="tpu_custom_call" | custom-call | tf_op jit(solution)/shard_map/prepare/pallas_call | solution.py:634
  2.3 20.1 %exchange_first.1 = (f32[3,128,256]{2,1,0:T(8,128)}, f32[8,128]{1,0:T(8,128)}) custom-call(f32[32,128]{1,0:T(8,128)} %get-tuple-element.33.scalars, f32[32,128,256]{2,1,0:T(8,128)} %nodes.1), custom_call_target="tpu_custom_call" | custom-call | tf_op jit(solution)/shard_map/exchange_first/pallas_call | solution.py:653
  22.4 8.9 %pass_first.1 = (f32[16,128,256]{2,1,0:T(8,128)}, f32[16,128,256]{2,1,0:T(8,128)}, f32[4,8,512]{2,1,0:T(8,128)}) custom-call(f32[32,128,256]{2,1,0:T(8,128)} %nodes.1, f32[3,128,256]{2,1,0:T(8,128)} %get-tuple-element.34.planes, f32[8,128]{1,0:T(8,128)} %get-tuple-element.35.most, f32[32,128]{1,0:T(8,128)} %get-tuple-element.33.scalars, ...), custom_call_target="tpu_custom_call" | custom-call | tf_op jit(solution)/shard_map/pass_first/pallas_call | solution.py:688
  31.3 3.3 %all-gather = f32[8,8,512]{2,1,0:T(8,128)} all-gather(f32[4,8,512]{2,1,0:T(8,128)} %get-tuple-element.40), channel_id=2, replica_groups=mesh['gx'=4,'gy'=4,'gz'=2] {'gz'}, dimensions={0}, use_global_device_ids=true | all-gather | bytes 196608 | tf_op jit(solution)/shard_map/all_gather | solution.py:715
  34.6 9.3 %pass_third.1 = (f32[16,128,128]{2,1,0:T(8,128)}, f32[1281,8,128]{2,1,0:T(8,128)}, s32[1]{0:T(128)}) custom-call(s32[1,512]{1,0:T(1,128)} %get-tuple-element.38.placed, f32[16,128,256]{2,1,0:T(8,128)} %get-tuple-element.39.coarse, f32[2,4,8,512]{3,2,1,0:T(8,128)} %bitcast.15, f32[8,128]{1,0:T(8,128)} %get-tuple-element.36.coefz, f32[128,128]{1,0:T(8,128)} %factor_z.3, ...), custom_call_target="tpu_custom_call" | custom-call | tf_op jit(solution)/shard_map/pass_third/pallas_call | solution.py:718
  44.5 69.5 %conditional.1 = (f32[1,8,128,2,4,128]{5,4,3,2,1,0:T(4,128)}) conditional(s32[]{:T(128)} %bitcast.10, f32[1281,8,128]{2,1,0:T(8,128)} %get-tuple-element.44, f32[1281,8,128]{2,1,0:T(8,128)} %get-tuple-element.44, f32[1281,8,128]{2,1,0:T(8,128)} %get-tuple-element.44, f32[1281,8,128]{2,1,0:T(8,128)} %get-tuple-element.44), branch_computations={%region_0.0_spmd, %region_1.0_spmd, %region_2.0_spmd, %region_3.0_... | conditional | bytes 8 | solution.py:620
  44.5 65.2 %spread.4 = (f32[8,128,8,128]{3,2,1,0:T(8,128)}, f32[4,257,8,128]{3,2,1,0:T(8,128)}) custom-call(f32[1281,8,128]{2,1,0:T(8,128)} %outgoing), custom_call_target="tpu_custom_call" | custom-call | tf_op jit(solution)/shard_map/cond/branch_0_fun/spread/pallas_call | solution.py:585
  109.7 4.3 %gather.4 = f32[8,128,8,128]{3,2,1,0:T(8,128)} custom-call(f32[8,128,8,128]{3,2,1,0:T(8,128)} %get-tuple-element.10.base, f32[4,257,8,128]{3,2,1,0:T(8,128)} %get-tuple-element.11.hbm_lists), custom_call_target="tpu_custom_call" | custom-call | tf_op jit(solution)/shard_map/cond/branch_0_fun/gather/pallas_call | solution.py:603
